TPU v7x, 256 devices: a whole 4x4x8 slice. The times are simulated.
256 devices in a mesh: fsdp: 16 (over y_lo, x, core), seq: 16 (over y_hi, z).
Axes of the slice: x: 4, y: 4 (y_hi: 2, y_lo: 2; y = y_hi * 2 + y_lo), z: 8, core: 2. Of those that a mesh axis runs over, the one named last changes fastest.
Arguments:
- primal: bfloat16 [4096, 5120], P('seq', 'fsdp'), may hold values from -6 to 6
- tangent: bfloat16 [4096, 5120], P('seq', 'fsdp'), may hold values from -6 to 6
- w_in: bfloat16 [5120, 13824], P('seq', 'fsdp'), may hold values from -0.078125 to 0.078125
- b_in: float32 [13824], P('fsdp'), may hold values from -3 to 3
- w_out: bfloat16 [13824, 5120], P('fsdp', 'seq'), may hold values from -0.0625 to 0.0625
- b_out: float32 [5120], replicated, may hold values from -3 to 3
- gate_mod: float32 [5120], replicated, may hold values from 0.5 to 1.5
- gate_tan: float32 [5120], replicated, may hold values from -3 to 3
Outputs:
- branch_out: bfloat16 [16, 256, 5120], P(None, 'fsdp', 'seq')
- branch_tan: bfloat16 [16, 256, 5120], P(None, 'fsdp', 'seq')
All inputs are finite; a program needn't handle non-finite values.
Results may differ from a plain program's by a relative error of at most 0.024.
Values may be sent and summed in bfloat16 or wider, within the bound.
A program may use at most 64 MiB of HBM per device.

v0:
```python
import jax
import jax.numpy as jnp
from jax import lax
from jax.sharding import PartitionSpec as P


def gelu_pair(pre):
    inner = 0.7978845608 * (pre + 0.044715 * pre * pre * pre)
    curve = jnp.tanh(inner)
    value = 0.5 * pre * (1.0 + curve)
    slope = 0.5 * (1.0 + curve) + 0.5 * pre * (1.0 - curve * curve) * 0.7978845608 * (
        1.0 + 3.0 * 0.044715 * pre * pre
    )
    return (value, slope)


def finish(totals, b_out, gate_mod, gate_tan, offset, width):
    bias = lax.dynamic_slice_in_dim(b_out, offset, width, 0)
    scale = lax.dynamic_slice_in_dim(gate_mod, offset, width, 0)
    scale_tan = lax.dynamic_slice_in_dim(gate_tan, offset, width, 0)
    shifted = totals[0] + bias
    out_part = scale * shifted
    tan_part = scale * totals[1] + scale_tan * shifted
    return jnp.stack([out_part, tan_part]).astype(jnp.bfloat16)


def shards(primal, tangent, w_in, b_in, w_out, b_out, gate_mod, gate_tan):
    rows = primal.shape[0]
    whole_p, whole_t = (
        lax.all_gather(primal, "fsdp", axis=1, tiled=True),
        lax.all_gather(tangent, "fsdp", axis=1, tiled=True),
    )
    stacked = jnp.concatenate([whole_p, whole_t], 0)
    summed = jnp.dot(
        stacked, lax.all_gather(w_in, "seq", axis=0, tiled=True), preferred_element_type=jnp.float32
    )
    value, slope = gelu_pair(summed[:rows] + b_in)
    hidden = jnp.concatenate(
        [value.astype(jnp.bfloat16), (slope * summed[rows:]).astype(jnp.bfloat16)], 0
    )
    partial_sum = jnp.dot(
        hidden, lax.all_gather(w_out, "seq", axis=1, tiled=True), preferred_element_type=jnp.float32
    ).reshape(2, rows, -1)
    full_width = partial_sum.shape[2]
    reduced = lax.psum_scatter(
        partial_sum.astype(jnp.bfloat16), "fsdp", scatter_dimension=2, tiled=True
    ).astype(jnp.float32)
    width = full_width // lax.axis_size("fsdp")
    finished = finish(reduced, b_out, gate_mod, gate_tan, lax.axis_index("fsdp") * width, width)
    result = lax.all_to_all(
        lax.all_to_all(finished[:, None], "fsdp", split_axis=2, concat_axis=3, tiled=True),
        "seq",
        split_axis=3,
        concat_axis=1,
        tiled=True,
    )
    return (result[0], result[1])


def solution(mesh):
    return jax.shard_map(
        shards,
        mesh=mesh,
        in_specs=(
            P("seq", "fsdp"),
            P("seq", "fsdp"),
            P("seq", "fsdp"),
            P("fsdp"),
            P("fsdp", "seq"),
            P(),
            P(),
            P(),
        ),
        out_specs=(P(None, "fsdp", "seq"), P(None, "fsdp", "seq")),
        check_vma=False,
    )
```

profile of v0, /device:TPU:1, one launch (start us, length us, event | category | flops | bytes accessed | tf_op | source)
XLA Modules:
  0.0 590.4 jit_solution(18204694395027653538)
XLA Ops:
  7.2 0.0 all-gather.5.cloned.1.call-start
  7.2 0.7 all-gather.5.cloned.1.call-update
  7.9 0.0 all-gather.7.cloned.1.call-start
  7.9 0.7 all-gather.7.cloned.1.call-update
  8.6 0.0 all-gather.9.cloned.1.call-start
  8.7 0.7 all-gather.9.cloned.1.call-update
  9.4 0.0 all-gather.11.cloned.1.call-start
  9.4 0.5 all-gather.11.cloned.1.call-update
  10.0 0.0 copy-start
  10.0 0.0 all-reduce.3.cloned.1.call-start
  10.0 41.5 %all-gather.5.cloned.1.call-done = bf16[256,5120]{0,1:T(8,128)(2,1)} async-done(((bf16[256,320]{0,1:T(8,128)(2,1)}), bf16[256,5120]{0,1:T(8,128)(2,1)}) %all-gather.5.cloned.1.call-update) | async-done | bytes 2621456 | tf_op jit(solution)/shard_map/all_gather | solution.py:30
  51.5 39.4 %all-gather.7.cloned.1.call-done = bf16[256,5120]{0,1:T(8,128)(2,1)} async-done(((bf16[256,320]{0,1:T(8,128)(2,1)}), bf16[256,5120]{0,1:T(8,128)(2,1)}) %all-gather.7.cloned.1.call-update) | async-done | bytes 2621456 | tf_op jit(solution)/shard_map/all_gather | solution.py:31
  90.8 145.6 %all-gather.9.cloned.1.call-done = bf16[5120,864]{1,0:T(8,128)(2,1)} async-done(((bf16[320,864]{1,0:T(8,128)(2,1)}), bf16[5120,864]{1,0:T(8,128)(2,1)}) %all-gather.9.cloned.1.call-update) | async-done | bytes 8847376 | tf_op jit(solution)/shard_map/all_gather | solution.py:35
  236.4 11.2 %fusion = f32[512,864]{0,1:T(8,128)S(1)} fusion(bf16[5120,864]{1,0:T(8,128)(2,1)} %all-gather.9.cloned.1.call-done, bf16[256,5120]{0,1:T(8,128)(2,1)} %all-gather.7.cloned.1.call-done, bf16[256,5120]{0,1:T(8,128)(2,1)} %all-gather.5.cloned.1.call-done), kind=kOutput, calls=%fused_computation.1 | convolution fusion | flops 4540334080 | bytes 15859712 | tf_op jit(solution)/shard_map/dot_general | solution.py:34
  247.7 0.0 copy-done
  247.7 0.7 multiply_convert_fusion
  248.4 131.0 %all-gather.11.cloned.1.call-done = bf16[864,5120]{0,1:T(8,128)(2,1)} async-done(((bf16[864,320]{0,1:T(8,128)(2,1)}), bf16[864,5120]{0,1:T(8,128)(2,1)}) %all-gather.11.cloned.1.call-update) | async-done | bytes 8847376 | tf_op jit(solution)/shard_map/all_gather | solution.py:42
  379.4 11.1 %convolution_convert_fusion = bf16[512,5120]{1,0:T(8,128)(2,1)} fusion(bf16[864,5120]{0,1:T(8,128)(2,1)} %all-gather.11.cloned.1.call-done, bf16[256,864]{0,1:T(8,128)(2,1)S(1)} %get-tuple-element.11, bf16[256,864]{0,1:T(8,128)(2,1)S(1)} %get-tuple-element.10), kind=kOutput, calls=%fused_computation | convolution fusion | flops 4534239232 | bytes 14974976 | tf_op jit(solution)/shard_map/dot_general | solution.py:41
  390.5 13.6 %copy.27 = bf16[2,256,5120]{1,0,2:T(2,128)(2,1)} copy(bf16[2,256,5120]{2,1,0:T(8,128)(2,1)} %bitcast.22) | data formatting | bytes 10485760 | tf_op jit(solution)/shard_map/convert_element_type | solution.py:46
  404.1 0.0 copy-start.1
  404.1 0.0 all-reduce.3.cloned.1.call-update
  404.1 0.8 dynamic_slice.10
  404.9 0.8 dynamic_slice.9
  405.7 0.8 dynamic_slice.11
  406.4 0.0 copy-done.1
  406.4 0.6 dynamic-slice
  407.7 130.7 %all-reduce.3.cloned.1.call-done = bf16[2,256,5120]{1,0,2:T(2,128)(2,1)} async-done(((bf16[2,256,5120]{1,0,2:T(2,128)(2,1)}), bf16[2,256,5120]{1,0,2:T(2,128)(2,1)}) %all-reduce.3.cloned.1.call-update) | async-done | bytes 5242896
  538.4 1.2 constant_dynamic-slice_fusion
  539.6 0.2 fusion.16
  539.9 0.5 copy.29
  540.3 14.2 %all_to_all.33 = bf16[2,1,256,320]{3,0,1,2:T(2,128)(2,1)S(1)} all-to-all(bf16[2,1,256,320]{3,0,1,2:T(2,128)(2,1)S(1)} %copy.29), channel_id=1, replica_groups=mesh['fsdp'=16,'seq'=16] {'fsdp'}, dimensions={2} | all-to-all | bytes 655360 | tf_op jit(solution)/shard_map/all_to_all | solution.py:51
  554.6 1.7 copy.36
  556.3 2.8 reshape.74
  559.1 19.6 %all_to_all.34 = bf16[16,2,5120]{2,1,0:T(2,128)(2,1)S(1)} all-to-all(bf16[16,2,5120]{2,1,0:T(2,128)(2,1)S(1)} %reshape.74), channel_id=1, replica_groups=mesh['fsdp'=16,'seq'=16] {'seq'}, dimensions={0} | all-to-all | bytes 655360 | tf_op jit(solution)/shard_map/all_to_all | solution.py:50
  578.7 1.9 reshape.75
  580.5 1.8 copy.37
  582.4 0.7 copy.35
  583.1 0.7 copy.34
  (4 shorter events, 0.2 us)
Async XLA Ops:
  7.2 44.3 %all-gather.5.cloned.1.call-start = ((), (), s32[]{:S(2)}) async-start(), calls=%async_computation.2 | async-start | bytes 2785280 | tf_op jit(solution)/shard_map/all_gather | solution.py:30
  7.9 82.9 %all-gather.7.cloned.1.call-start = ((), (), s32[]{:S(2)}) async-start(), calls=%async_computation.3 | async-start | bytes 2785280 | tf_op jit(solution)/shard_map/all_gather | solution.py:31
  8.6 227.8 %all-gather.9.cloned.1.call-start = ((), (), s32[]{:S(2)}) async-start(), calls=%async_computation.4 | async-start | bytes 9748480 | tf_op jit(solution)/shard_map/all_gather | solution.py:35
  9.4 370.0 %all-gather.11.cloned.1.call-start = ((), (), s32[]{:S(2)}) async-start(), calls=%async_computation.5 | async-start | bytes 9748480 | tf_op jit(solution)/shard_map/all_gather | solution.py:42
  10.0 237.8 %copy-start = (f32[864]{0:T(1024)S(1)}, f32[864]{0:T(1024)}, u32[]{:S(2)}) copy-start(f32[864]{0:T(1024)} %param.11) | copy-start | bytes 10372
  10.0 528.4 %all-reduce.3.cloned.1.call-start = ((), (), s32[]{:S(2)}) async-start(), calls=%async_computation.6 | async-start | bytes 10485760
  404.1 2.4 copy-start.1
Sparse Core Ops, SparseCore 0:
  9.8 41.5 all-gather.4
  53.3 37.4 all-gather.6
  93.4 142.9 all-gather.8
  238.9 140.4 all-gather.10
  404.2 134.0 all-reduce.2
where the time goes:
time: 592 us; the launch traced here: 590 us
  waiting for transfers between devices  491 us (83%)
  blocking collectives  33.8 us (6%)
  local copies, waits for them, and re-layouts  27.9 us (5%)
  matrix products  22.4 us (4%)
  between operations  14.6 us (2%)
    all_gather x1, waiting for transfers between devices, shards(): lax.all_gather(w_in, 'seq', axis=0, tiled=True)  146 us
    unnamed x6, waiting for transfers between devices  133 us
    all_gather x1, waiting for transfers between devices, shards(): lax.all_gather(w_out, 'seq', axis=1, tiled=True)  131 us
    all_gather x1, waiting for transfers between devices, shards(): lax.all_gather(primal, 'fsdp', axis=1, tiled=True)  41.5 us
    all_gather x1, waiting for transfers between devices, shards(): lax.all_gather(tangent, 'fsdp', axis=1, tiled=True)  39.4 us
    all_to_all x1, blocking collectives, shards(): lax.all_to_all(lax.all_to_all(finished[:, None], 'fsdp', split_axis=2, co...  19.6 us
    all_to_all x1, blocking collectives, shards(): lax.all_to_all(finished[:, None], 'fsdp', split_axis=2, concat_axis=3, ti...  14.2 us
    convert_element_type x1, local copies, waits for them, and re-layouts, shards(): partial_sum.astype(jnp.bfloat16)  13.6 us
  transfers between devices with their start and end apart: 5, of which 5 were waited for; matrix products, arithmetic and copies ran while one was open for 3% of the time, Pallas kernels for 0%

commit v1 on v0

v1 whole, which is shorter than its diff:
```python
import functools

import jax
import jax.numpy as jnp
from jax import lax
from jax.experimental import pallas as pl
from jax.experimental.pallas import tpu as pltpu
from jax.sharding import PartitionSpec as P

MESH = pl.DeviceIdType.MESH
ORDER = (0, 1, 7, 2, 6, 3, 5, 4)


def gelu_pair(pre):
    inner = 0.7978845608 * (pre + 0.044715 * pre * pre * pre)
    curve = jnp.tanh(inner)
    value = 0.5 * pre * (1.0 + curve)
    slope = 0.5 * (1.0 + curve) + 0.5 * pre * (1.0 - curve * curve) * 0.7978845608 * (
        1.0 + 3.0 * 0.044715 * pre * pre
    )
    return value, slope


def reach(q, way):
    return 4 if (q == 0) == (way == 1) else 3


def kernel(
    x_in, w_in, b_in, gates,
    out_p, out_t,
    wbuf, xbuf, bias, acc, hid, part, r1x, r1y, s2x, s2y, r2x, r2y, fin, land,
    swap_s, swap_r, bias_s, bias_r, ring_s, ring_r, sib_s, sib_r,
    xs1_s, xs1_r, xs2_s, xs2_r, rs1_s, rs1_r, rs2_s, rs2_r, fin_s, fin_r,
):
    f = lax.axis_index("fsdp")
    s = lax.axis_index("seq")
    core = lax.rem(f, 2)
    x = lax.rem(f // 2, 4)
    y_lo = f // 8
    y_hi = s // 8
    z = lax.rem(s, 8)
    y = y_hi * 2 + y_lo
    sends = []

    def dev(xx, yy, zz, cc):
        return (lax.rem(yy, 2) * 8 + xx * 2 + cc, (yy // 2) * 8 + zz)

    def at(dx=0, dy=0, dz=0, flip=False):
        return dev(
            lax.rem(x + dx + 4, 4), lax.rem(y + dy + 4, 4), lax.rem(z + dz + 8, 8),
            1 - core if flip else core,
        )

    def copy(src, dst, ssem, rsem, where):
        return pltpu.make_async_remote_copy(
            src_ref=src, dst_ref=dst, send_sem=ssem, recv_sem=rsem, device_id=where, device_id_type=MESH
        )

    def send(src, dst, ssem, rsem, where):
        c = copy(src, dst, ssem, rsem, where)
        c.start()
        sends.append(c)

    def arrived(dst, ssem, rsem, where):
        copy(dst, dst, ssem, rsem, where).wait_recv()

    barrier = pltpu.get_barrier_semaphore()
    friends = [at(dz=d, flip=fl) for d in range(8) for fl in (False, True) if d or fl]
    friends += [at(dx=d) for d in (1, 2, 3)] + [at(dy=d) for d in (1, 2, 3)] + [at(dy=2, flip=True)]
    for who in friends:
        pl.semaphore_signal(barrier, inc=1, device_id=who, device_id_type=MESH)
    pl.semaphore_wait(barrier, len(friends))

    me_k = (y_lo * 4 + x) * 2 + y_hi
    rows = lambda q: pl.ds(q * 160, 160)
    half = lambda a: pl.ds(a * 128, 128)
    stays = y_hi == core
    partner = at(dy=2, flip=True)
    pieces = []
    for h in range(2):
        for q in range(2):
            pieces.append((w_in.at[h, rows(q)], wbuf.at[h, 0, core, rows(q)], wbuf.at[h, 0, 1 - core, rows(q)]))
    other_k = (y_lo * 4 + x) * 2 + core
    xp = [(x_in.at[half(a)], xbuf.at[me_k, half(a)], xbuf.at[(y_lo * 4 + x) * 2 + 1 - y_hi, half(a)]) for a in range(2)]
    pieces = [pieces[0], pieces[1], xp[0], xp[1], pieces[2], pieces[3]]

    @pl.when(stays)
    def _():
        for i, (src, dst, _away) in enumerate(pieces):
            pltpu.make_async_copy(src, dst, swap_r.at[i]).start()

    @pl.when(jnp.logical_not(stays))
    def _():
        for i, (src, _dst, away) in enumerate(pieces):
            copy(src, away, swap_s.at[i], swap_r.at[i], partner).start()

    send(b_in, bias.at[core], bias_s, bias_r, at(flip=True))
    bias[core] = b_in[...]

    def own(i):
        src, dst, _ = pieces[i]
        pltpu.make_async_copy(src, dst, swap_r.at[i]).wait()

    def w_at(h, delta, q, who=None):
        return wbuf.at[h, delta % 8, core if who is None else who, rows(q)]

    def ring_send(h, q, way, d):
        send(
            w_at(h, -way * (d - 1), q), w_at(h, -way * d, q),
            ring_s.at[h, q, (way + 1) // 2, d - 1], ring_r.at[h, q, (way + 1) // 2, d - 1], at(dz=way),
        )

    def sib_send(h, q, delta):
        send(w_at(h, delta, q), w_at(h, delta, q), sib_s.at[h, q, delta % 8], sib_r.at[h, q, delta % 8], at(flip=True))

    def sib_wait(h, delta):
        for q in range(2):
            arrived(w_at(h, delta, q, 1 - core), sib_s.at[h, q, delta % 8], sib_r.at[h, q, delta % 8], at(flip=True))

    def ring_step(h, d):
        for q in range(2):
            for way in (1, -1):
                if d > reach(q, way):
                    continue
                arrived(
                    w_at(h, -way * d, q),
                    ring_s.at[h, q, (way + 1) // 2, d - 1], ring_r.at[h, q, (way + 1) // 2, d - 1], at(dz=way),
                )
                if d < reach(q, way):
                    ring_send(h, q, way, d + 1)
                sib_send(h, q, -way * d)

    def ring_open(h, q, i):
        own(i)
        for way in (1, -1):
            ring_send(h, q, way, 1)
        sib_send(h, q, 0)

    def x_slot(a, dx, dy):
        xx, yy = lax.rem(x + dx + 8, 4), lax.rem(y + dy + 8, 4)
        return xbuf.at[(lax.rem(yy, 2) * 4 + xx) * 2 + yy // 2, half(a)]

    def x_first(a, d):
        return (d, 0) if a == 0 else (0, d)

    ring_open(0, 0, 0)
    ring_open(0, 1, 1)
    for a in range(2):
        own(2 + a)
        for d in (1, 2, 3):
            dx, dy = x_first(a, d)
            send(x_slot(a, 0, 0), x_slot(a, 0, 0), xs1_s.at[a, d - 1], xs1_r.at[a, d - 1], at(dx, dy))
    acc[...] = jnp.zeros_like(acc)
    own(4)
    own(5)

    def x_second(a, r, d):
        dx, dy = x_first(1 - a, d)
        sx, sy = x_first(a, -r)
        send(x_slot(a, sx, sy), x_slot(a, sx, sy), xs2_s.at[a, r, d - 1], xs2_r.at[a, r, d - 1], at(dx, dy))

    def x_arrive(a, r):
        for d in (1, 2, 3):
            dx, dy = x_first(1 - a, -d)
            sx, sy = x_first(a, -r)
            arrived(x_slot(a, dx + sx, dy + sy), xs2_s.at[a, r, d - 1], xs2_r.at[a, r, d - 1], at(dx, dy))

    for a in range(2):
        for d in (1, 2, 3):
            x_second(a, 0, d)
    ring_step(0, 1)
    for r in (1, 3, 2):
        for a in range(2):
            sx, sy = x_first(a, -r)
            arrived(x_slot(a, sx, sy), xs1_s.at[a, r - 1], xs1_r.at[a, r - 1], at(sx, sy))
            for d in (1, 2, 3):
                x_second(a, r, d)
    ring_step(0, 2)
    ring_step(0, 3)
    for q in range(2):
        for way in (1, -1):
            ring_send(1, q, way, 1)
        sib_send(1, q, 0)
    ring_step(0, 4)
    for a in range(2):
        for r in range(4):
            x_arrive(a, r)
    for delta in ORDER:
        sib_wait(0, delta)
    arrived(bias.at[1 - core], bias_s, bias_r, at(flip=True))

    def first(i, carry):
        delta, h = i // 2, lax.rem(i, 2)
        k = h * 8 + lax.rem(z + delta, 8)
        w = wbuf[0, delta, h]
        xk = xbuf[k]
        acc[0] += jnp.dot(xk[:, :320], w, preferred_element_type=jnp.float32)
        acc[1] += jnp.dot(xk[:, 320:], w, preferred_element_type=jnp.float32)
        return carry

    lax.fori_loop(0, 16, first, 0)

    def activate(i, carry):
        r = pl.ds(pl.multiple_of(i * 32, 32), 32)
        into = pl.ds(pl.multiple_of(lax.rem(i, 4) * 32, 32), 32)
        value, slope = gelu_pair(acc[0, r, :] + bias[y_hi])
        hid[i // 4, 0, into, :] = value.astype(jnp.bfloat16)
        hid[i // 4, 1, into, :] = (slope * acc[1, r, :]).astype(jnp.bfloat16)
        return carry

    lax.fori_loop(0, 8, activate, 0)

    def second(i):
        delta = ORDER[i]

        def body(j, carry):
            h, yl = j // 2, lax.rem(j, 2)
            both = lax.dot_general(
                hid[yl].reshape(256, 864), wbuf[1, delta, h], (((1,), (1,)), ((), ())),
                preferred_element_type=jnp.float32,
            )
            packed = jnp.concatenate([both[:128], both[128:]], axis=1).astype(jnp.bfloat16)
            for b in range(8):
                part[i, b % 2, h, yl, b // 2] = packed[b * 16 : (b + 1) * 16]
            return carry

        lax.fori_loop(0, 4, body, 0)
        for d in (1, 2, 3):
            xx = lax.rem(x + d, 4)
            send(part.at[i, 0, :, :, xx], r1x.at[i, d - 1], rs1_s.at[i, 0, d - 1], rs1_r.at[i, 0, d - 1], at(dx=d))
            yy = lax.rem(y + d, 4)
            send(
                part.at[i, 1, yy // 2, lax.rem(yy, 2)], r1y.at[i, d - 1],
                rs1_s.at[i, 1, d - 1], rs1_r.at[i, 1, d - 1], at(dy=d),
            )

    f32 = lambda v: v.astype(jnp.float32)

    def reduce_one(i):
        for d in (1, 2, 3):
            arrived(r1x.at[i, d - 1], rs1_s.at[i, 0, d - 1], rs1_r.at[i, 0, d - 1], at(dx=-d))
        for h in range(2):
            for yl in range(2):
                t = f32(part[i, 0, h, yl, x])
                for d in range(3):
                    t += f32(r1x[i, d, h, yl])
                s2x[i, h, yl] = t.astype(jnp.bfloat16)
        for d in (1, 2, 3):
            yy = lax.rem(y + d, 4)
            send(
                s2x.at[i, yy // 2, lax.rem(yy, 2)], r2x.at[i, d - 1],
                rs2_s.at[i, 0, d - 1], rs2_r.at[i, 0, d - 1], at(dy=d),
            )
        for d in (1, 2, 3):
            arrived(r1y.at[i, d - 1], rs1_s.at[i, 1, d - 1], rs1_r.at[i, 1, d - 1], at(dy=-d))
        for b in range(4):
            t = f32(part[i, 1, y_hi, y_lo, b])
            for d in range(3):
                t += f32(r1y[i, d, b])
            s2y[i, b] = t.astype(jnp.bfloat16)
        for d in (1, 2, 3):
            send(s2y.at[i, lax.rem(x + d, 4)], r2y.at[i, d - 1], rs2_s.at[i, 1, d - 1], rs2_r.at[i, 1, d - 1], at(dx=d))

    def reduce_two(i):
        delta = ORDER[i]
        g = gates[y_hi * 8 + lax.rem(z + delta, 8)]
        for d in (1, 2, 3):
            arrived(r2x.at[i, d - 1], rs2_s.at[i, 0, d - 1], rs2_r.at[i, 0, d - 1], at(dy=-d))
            arrived(r2y.at[i, d - 1], rs2_s.at[i, 1, d - 1], rs2_r.at[i, 1, d - 1], at(dx=-d))
        for cc in range(2):
            t = f32(s2x[i, y_hi, y_lo]) if cc == 0 else f32(s2y[i, x])
            for d in range(3):
                t += f32((r2x, r2y)[cc][i, d])
            shifted = t[:, :320] + g[0:1]
            fin[i, cc, 0] = (g[1:2] * shifted).astype(jnp.bfloat16)
            fin[i, cc, 1] = (g[1:2] * t[:, 320:] + g[2:3] * shifted).astype(jnp.bfloat16)
        if i:
            send(fin.at[i, core], land.at[i, 0], fin_s.at[i, 0], fin_r.at[i, 0], at(dz=delta))
        send(fin.at[i, 1 - core], land.at[i, 1], fin_s.at[i, 1], fin_r.at[i, 1], at(dz=delta, flip=True))

    groups = ((0,), (1, 2), (3, 4), (5, 6), (7,))
    for d in range(5):
        if d:
            ring_step(1, d)
        for i in groups[d]:
            sib_wait(1, ORDER[i])
            second(i)
        if d >= 1:
            for i in groups[d - 1]:
                reduce_one(i)
        if d >= 2:
            for i in groups[d - 2]:
                reduce_two(i)
    for i in groups[3]:
        reduce_two(i)
    for i in groups[4]:
        reduce_one(i)
    for i in groups[4]:
        reduce_two(i)

    for i in range(8):
        delta = ORDER[i]
        zz = lax.rem(z - delta + 8, 8)
        for other in range(2):
            cc = 1 - core if other else core
            if i or other:
                arrived(land.at[i, other], fin_s.at[i, other], fin_r.at[i, other], at(dz=-delta, flip=bool(other)))
                src = land[i, other]
            else:
                src = fin[i, core]
            out_p[cc * 8 + zz] = src[0]
            out_t[cc * 8 + zz] = src[1]

    @pl.when(jnp.logical_not(stays))
    def _():
        for i, (src, _dst, away) in enumerate(pieces):
            copy(src, away, swap_s.at[i], swap_r.at[i], partner).wait_send()

    for c in sends:
        c.wait_send()


def shards(primal, tangent, w_in, b_in, w_out, b_out, gate_mod, gate_tan):
    x_in = jnp.concatenate([primal, tangent], 1)
    w = jnp.stack([w_in, w_out.T])
    gates = jnp.stack([b_out, gate_mod, gate_tan]).reshape(3, 16, 320).transpose(1, 0, 2)
    bf, dma = jnp.bfloat16, pltpu.SemaphoreType.DMA
    both = lambda *shape: [dma(shape), dma(shape)]
    return pl.pallas_call(
        kernel,
        out_shape=[jax.ShapeDtypeStruct((16, 16, 320), bf)] * 2,
        in_specs=[pl.BlockSpec(memory_space=pltpu.VMEM)] * 4,
        out_specs=[pl.BlockSpec(memory_space=pltpu.VMEM)] * 2,
        scratch_shapes=[
            pltpu.VMEM((2, 8, 2, 320, 864), bf),
            pltpu.VMEM((16, 256, 640), bf),
            pltpu.VMEM((2, 1, 864), jnp.float32),
            pltpu.VMEM((2, 256, 864), jnp.float32),
            pltpu.VMEM((2, 2, 128, 864), bf),
            pltpu.VMEM((8, 2, 2, 2, 4, 16, 640), bf),
            pltpu.VMEM((8, 3, 2, 2, 16, 640), bf),
            pltpu.VMEM((8, 3, 4, 16, 640), bf),
            pltpu.VMEM((8, 2, 2, 16, 640), bf),
            pltpu.VMEM((8, 4, 16, 640), bf),
            pltpu.VMEM((8, 3, 16, 640), bf),
            pltpu.VMEM((8, 3, 16, 640), bf),
            pltpu.VMEM((8, 2, 2, 16, 320), bf),
            pltpu.VMEM((8, 2, 2, 16, 320), bf),
            *both(6), dma, dma, *both(2, 2, 2, 4), *both(2, 2, 8),
            *both(2, 3), *both(2, 4, 3), *both(8, 2, 3), *both(8, 2, 3), *both(8, 2),
        ],
        compiler_params=pltpu.CompilerParams(
            collective_id=0, has_side_effects=True, vmem_limit_bytes=56 << 20
        ),
        cost_estimate=pl.CostEstimate(flops=9 * 10**9, bytes_accessed=3 * 10**6, transcendentals=221184),
        name="ffn_pair",
    )(x_in, w, b_in.reshape(1, 864), gates)


def solution(mesh):
    return jax.shard_map(
        shards,
        mesh=mesh,
        in_specs=(
            P("seq", "fsdp"),
            P("seq", "fsdp"),
            P("seq", "fsdp"),
            P("fsdp"),
            P("fsdp", "seq"),
            P(),
            P(),
            P(),
        ),
        out_specs=(P(None, "fsdp", "seq"), P(None, "fsdp", "seq")),
        check_vma=False,
    )
```

time: 592 us -> 167 us (0.28)
  waiting for transfers between devices: 491 us -> 0 us
  Pallas kernels: 0 us -> 154 us
  blocking collectives: 33.8 us -> 0 us
  matrix products: 22.4 us -> 0 us
  local copies, waits for them, and re-layouts: 27.9 us -> 9.21 us
  between operations: 14.6 us -> 0.68 us
    all_gather x4 -> x0, waiting for transfers between devices: 357 us -> none  [the longest x1 146 us: shards(): lax.all_gather(w_in, 'seq', axis=0, tiled=True)]
    pallas_call x0 -> x1, Pallas kernels: none -> 154 us  [shards(): pl.pallas_call(kernel, out_shape=[jax.ShapeDtypeStruct((16, 16, 320), bf)...]
    unnamed x6 -> x0, waiting for transfers between devices: 133 us -> none
    all_to_all x2 -> x0, blocking collectives: 33.8 us -> none  [the longest x1 19.6 us: shards(): lax.all_to_all(lax.all_to_all(finished[:, None], 'fsdp', split_axis=2, co...]
    dot_general x2 -> x0, matrix products: 22.4 us -> none  [the longest x1 11.2 us: shards(): jnp.dot(stacked, lax.all_gather(w_in, 'seq', axis=0, tiled=True), preferr...]
    convert_element_type x1 -> x0, local copies, waits for them, and re-layouts: 13.6 us -> none  [shards(): partial_sum.astype(jnp.bfloat16)]
  transfers between devices with their start and end apart: 5 -> 0, of which waited for: 5 -> 0; matrix products, arithmetic and copies ran while one was open for 3% -> 0% of each run, Pallas kernels for 0% -> 0%
where the time goes in v1:
time: 167 us; the launch traced here: 166 us
  Pallas kernels  154 us (92%)
  local copies, waits for them, and re-layouts  9.21 us (6%)
  other arithmetic  2.74 us (2%)
    pallas_call x1, Pallas kernels, shards(): pl.pallas_call(kernel, out_shape=[jax.ShapeDtypeStruct((16, 16, 320), bf)...  154 us
    unnamed x8, local copies, waits for them, and re-layouts  5.41 us

profile of v1, /device:TPU:1, one launch (start us, length us, event | category | flops | bytes accessed | tf_op | source)
XLA Modules:
  0.0 166.4 jit_solution(1752748354896105365)
XLA Ops:
  0.6 0.0 copy-start
  0.6 0.0 copy-start.1
  0.7 1.4 reshape.14.b_in
  2.0 0.8 stack.24
  2.8 0.8 stack.25
  3.6 0.8 stack.26
  4.5 0.7 maximum_bitcast_fusion.gates
  5.2 1.1 copy.10
  6.3 1.1 copy.11
  7.3 0.9 pad_maximum_fusion.1.x_in
  8.2 0.0 copy-done
  8.2 0.0 copy-done.1
  8.2 1.1 pad_maximum_fusion.w_in
  9.4 153.7 %ffn_pair.1 = (bf16[16,16,320]{2,1,0:T(8,128)(2,1)}, bf16[16,16,320]{2,1,0:T(8,128)(2,1)}) custom-call(bf16[256,640]{1,0:T(8,128)(2,1)} %pad_maximum_fusion.1.x_in, bf16[2,320,864]{2,1,0:T(8,128)(2,1)} %pad_maximum_fusion.w_in, f32[1,864]{1,0:T(1,128)} %reshape.14.b_in, f32[16,3,320]{2,1,0:T(4,128)} %maximum_bitcast_fusion.gates), custom_call_target="tpu_custom_call" | custom-call | flops 8999999488 | bytes 3000000 | tf_op jit(solution)/shard_map/ffn_pair/pallas_call | solution.py:329
  163.1 1.6 copy.14
  164.7 1.6 copy.15
Async XLA Ops:
  0.6 7.6 %copy-start = (bf16[864,320]{0,1:T(8,128)(2,1)S(1)}, bf16[864,320]{0,1:T(8,128)(2,1)}, u32[]{:S(2)}) copy-start(bf16[864,320]{0,1:T(8,128)(2,1)} %param.12) | copy-start | bytes 1658884
  0.6 7.6 %copy-start.1 = (bf16[320,864]{1,0:T(8,128)(2,1)S(1)}, bf16[320,864]{1,0:T(8,128)(2,1)}, u32[]{:S(2)}) copy-start(bf16[320,864]{1,0:T(8,128)(2,1)} %param.10) | copy-start | bytes 1658884

commit v2 on v1

--- a/solution.py
+++ b/solution.py
@@ -25,12 +25,16 @@
     return 4 if (q == 0) == (way == 1) else 3
 
 
+OFF = (0, -1, 1, 2)
+
+
 def kernel(
-    x_in, w_in, b_in, gates,
+    xp_in, xt_in, w_in, w_out, b_in, b_out, gate_mod, gate_tan,
     out_p, out_t,
-    wbuf, xbuf, bias, acc, hid, part, r1x, r1y, s2x, s2y, r2x, r2y, fin, land,
-    swap_s, swap_r, bias_s, bias_r, ring_s, ring_r, sib_s, sib_r,
-    xs1_s, xs1_r, xs2_s, xs2_r, rs1_s, rs1_r, rs2_s, rs2_r, fin_s, fin_r,
+    wbuf, xbuf, relay_w, relay_x, bias, gates, acc, hid,
+    part, r1x, r1y, s2x, s2y, r2x, r2y, fin, land,
+    swap_s, swap_r, relay_s, relay_r, bias_s, bias_r, ring_s, ring_r, sib_s, sib_r,
+    xs_s, xs_r, xf_s, xf_r, rs1_s, rs1_r, rs2_s, rs2_r, fin_s, fin_r,
 ):
     f = lax.axis_index("fsdp")
     s = lax.axis_index("seq")
@@ -66,40 +70,52 @@
 
     barrier = pltpu.get_barrier_semaphore()
     friends = [at(dz=d, flip=fl) for d in range(8) for fl in (False, True) if d or fl]
-    friends += [at(dx=d) for d in (1, 2, 3)] + [at(dy=d) for d in (1, 2, 3)] + [at(dy=2, flip=True)]
+    friends += [at(dx=d) for d in (1, 2, 3)] + [at(dy=d) for d in (1, 2, 3)]
+    friends += [at(dy=d, flip=True) for d in (1, 3)]
     for who in friends:
         pl.semaphore_signal(barrier, inc=1, device_id=who, device_id_type=MESH)
     pl.semaphore_wait(barrier, len(friends))
 
-    me_k = (y_lo * 4 + x) * 2 + y_hi
     rows = lambda q: pl.ds(q * 160, 160)
-    half = lambda a: pl.ds(a * 128, 128)
     stays = y_hi == core
-    partner = at(dy=2, flip=True)
-    pieces = []
-    for h in range(2):
-        for q in range(2):
-            pieces.append((w_in.at[h, rows(q)], wbuf.at[h, 0, core, rows(q)], wbuf.at[h, 0, 1 - core, rows(q)]))
-    other_k = (y_lo * 4 + x) * 2 + core
-    xp = [(x_in.at[half(a)], xbuf.at[me_k, half(a)], xbuf.at[(y_lo * 4 + x) * 2 + 1 - y_hi, half(a)]) for a in range(2)]
-    pieces = [pieces[0], pieces[1], xp[0], xp[1], pieces[2], pieces[3]]
-
-    @pl.when(stays)
-    def _():
-        for i, (src, dst, _away) in enumerate(pieces):
-            pltpu.make_async_copy(src, dst, swap_r.at[i]).start()
-
-    @pl.when(jnp.logical_not(stays))
-    def _():
-        for i, (src, _dst, away) in enumerate(pieces):
-            copy(src, away, swap_s.at[i], swap_r.at[i], partner).start()
-
-    send(b_in, bias.at[core], bias_s, bias_r, at(flip=True))
-    bias[core] = b_in[...]
+    moves = jnp.logical_not(stays)
+    own_k = (y_lo * 4 + x) * 2 + y_hi
+    sources = [w_in.at[rows(0)], w_in.at[rows(1)], xp_in, xt_in, w_out.at[rows(0)], w_out.at[rows(1)]]
+    homes = [
+        wbuf.at[0, 0, core, rows(0)], wbuf.at[0, 0, core, rows(1)], xbuf.at[own_k, 0], xbuf.at[own_k, 1],
+        wbuf.at[1, 0, core, rows(0)], wbuf.at[1, 0, core, rows(1)],
+    ]
+    relays = [relay_w.at[0], relay_w.at[0], relay_x, relay_x, relay_w.at[1], relay_w.at[1]]
+    passes = [(lax.rem(y + (3 if e == 0 else 1), 4) // 2) == core for e in range(2)]
+    step_of = lambda i: 1 if i % 2 == 0 else -1
+
+    def swap_copy(i):
+        return copy(sources[i], relays[i], swap_s.at[i], swap_r.at[i], at(dy=step_of(i), flip=True))
+
+    def relay_copy(i):
+        yy = lax.rem(y + step_of(i) + 4, 4)
+        k = (lax.rem(yy, 2) * 4 + x) * 2 + yy // 2
+        dst = xbuf.at[k, i % 2] if i in (2, 3) else homes[i]
+        return copy(relays[i], dst, relay_s.at[i], relay_r.at[i], at(dy=step_of(i)))
+
+    def swap_open(i):
+        @pl.when(stays)
+        def _():
+            pltpu.make_async_copy(sources[i], homes[i], relay_r.at[i]).start()
+
+        @pl.when(moves)
+        def _():
+            swap_copy(i).start()
+
+    def swap_pass(i):
+        for e in range(2):
+            @pl.when(passes[e])
+            def _():
+                swap_copy(i + e).wait_recv()
+                relay_copy(i + e).start()
 
     def own(i):
-        src, dst, _ = pieces[i]
-        pltpu.make_async_copy(src, dst, swap_r.at[i]).wait()
+        pltpu.make_async_copy(sources[i], homes[i], relay_r.at[i]).wait()
 
     def w_at(h, delta, q, who=None):
         return wbuf.at[h, delta % 8, core if who is None else who, rows(q)]
@@ -130,61 +146,88 @@
                     ring_send(h, q, way, d + 1)
                 sib_send(h, q, -way * d)
 
-    def ring_open(h, q, i):
-        own(i)
+    def ring_open(h, q):
         for way in (1, -1):
             ring_send(h, q, way, 1)
         sib_send(h, q, 0)
 
-    def x_slot(a, dx, dy):
-        xx, yy = lax.rem(x + dx + 8, 4), lax.rem(y + dy + 8, 4)
-        return xbuf.at[(lax.rem(yy, 2) * 4 + xx) * 2 + yy // 2, half(a)]
-
-    def x_first(a, d):
-        return (d, 0) if a == 0 else (0, d)
-
-    ring_open(0, 0, 0)
-    ring_open(0, 1, 1)
+    def slot(a, o1, o2, part_of=None):
+        dx, dy = (o1, o2) if a == 0 else (o2, o1)
+        xx, yy = lax.rem(x + dx + 4, 4), lax.rem(y + dy + 4, 4)
+        k = (lax.rem(yy, 2) * 4 + xx) * 2 + yy // 2
+        return xbuf.at[k, a] if part_of is None else xbuf.at[k, a, rows(part_of)]
+
+    def along(a, stage, d):
+        return at(dx=d) if (a == 0) == (stage == 0) else at(dy=d)
+
+    def offset(stage, r, d):
+        return (d, 0) if stage == 0 else (OFF[r], d)
+
+    def bc_open(a, stage, r=0):
+        for wi, way in enumerate((1, -1)):
+            src = slot(a, *offset(stage, r, 0))
+            i = stage * 4 + r
+            send(src, src, xs_s.at[a, i, wi], xs_r.at[a, i, wi], along(a, stage, way))
+
+    def bc_pass(a, stage, r=0):
+        for wi, way in enumerate((1, -1)):
+            i = stage * 4 + r
+            place = offset(stage, r, -way)
+            arrived(slot(a, *place), xs_s.at[a, i, wi], xs_r.at[a, i, wi], along(a, stage, way))
+            piece = slot(a, *place, wi)
+            send(piece, piece, xf_s.at[a, i, wi], xf_r.at[a, i, wi], along(a, stage, way))
+
+    def bc_end(a, stage, r=0):
+        for wi, way in enumerate((1, -1)):
+            i = stage * 4 + r
+            arrived(slot(a, *offset(stage, r, 2), wi), xf_s.at[a, i, wi], xf_r.at[a, i, wi], along(a, stage, way))
+
+    for i in range(4):
+        swap_open(i)
+    bias[core] = b_in[...].reshape(1, 864)
+    send(bias.at[core], bias.at[core], bias_s, bias_r, at(flip=True))
+    swap_pass(0)
+    for q in range(2):
+        own(q)
+        ring_open(0, q)
+    swap_pass(2)
     for a in range(2):
         own(2 + a)
-        for d in (1, 2, 3):
-            dx, dy = x_first(a, d)
-            send(x_slot(a, 0, 0), x_slot(a, 0, 0), xs1_s.at[a, d - 1], xs1_r.at[a, d - 1], at(dx, dy))
+        bc_open(a, 0)
+        bc_open(a, 1, 0)
     acc[...] = jnp.zeros_like(acc)
-    own(4)
-    own(5)
-
-    def x_second(a, r, d):
-        dx, dy = x_first(1 - a, d)
-        sx, sy = x_first(a, -r)
-        send(x_slot(a, sx, sy), x_slot(a, sx, sy), xs2_s.at[a, r, d - 1], xs2_r.at[a, r, d - 1], at(dx, dy))
-
-    def x_arrive(a, r):
-        for d in (1, 2, 3):
-            dx, dy = x_first(1 - a, -d)
-            sx, sy = x_first(a, -r)
-            arrived(x_slot(a, dx + sx, dy + sy), xs2_s.at[a, r, d - 1], xs2_r.at[a, r, d - 1], at(dx, dy))
-
+    for n, table in enumerate((b_out, gate_mod, gate_tan)):
+        for i in range(16):
+            first_row, lane = i * 320 // 128, i * 320 % 128
+            flat = jnp.concatenate([table[first_row + j : first_row + j + 1, :] for j in range(3)], axis=1)
+            gates[i, n : n + 1] = flat[:, lane : lane + 320]
+    ring_step(0, 1)
     for a in range(2):
-        for d in (1, 2, 3):
-            x_second(a, 0, d)
-    ring_step(0, 1)
-    for r in (1, 3, 2):
+        bc_pass(a, 0)
+        for r in (1, 2):
+            bc_open(a, 1, r)
+    for a in range(2):
+        bc_pass(a, 1, 0)
+    for a in range(2):
+        bc_end(a, 0)
+        bc_open(a, 1, 3)
+    for i in (4, 5):
+        swap_open(i)
+    ring_step(0, 2)
+    for r in (1, 2):
         for a in range(2):
-            sx, sy = x_first(a, -r)
-            arrived(x_slot(a, sx, sy), xs1_s.at[a, r - 1], xs1_r.at[a, r - 1], at(sx, sy))
-            for d in (1, 2, 3):
-                x_second(a, r, d)
-    ring_step(0, 2)
+            bc_pass(a, 1, r)
+    swap_pass(4)
+    for a in range(2):
+        bc_pass(a, 1, 3)
     ring_step(0, 3)
     for q in range(2):
-        for way in (1, -1):
-            ring_send(1, q, way, 1)
-        sib_send(1, q, 0)
+        own(4 + q)
+        ring_open(1, q)
+    for r in range(4):
+        for a in range(2):
+            bc_end(a, 1, r)
     ring_step(0, 4)
-    for a in range(2):
-        for r in range(4):
-            x_arrive(a, r)
     for delta in ORDER:
         sib_wait(0, delta)
     arrived(bias.at[1 - core], bias_s, bias_r, at(flip=True))
@@ -193,9 +236,8 @@
         delta, h = i // 2, lax.rem(i, 2)
         k = h * 8 + lax.rem(z + delta, 8)
         w = wbuf[0, delta, h]
-        xk = xbuf[k]
-        acc[0] += jnp.dot(xk[:, :320], w, preferred_element_type=jnp.float32)
-        acc[1] += jnp.dot(xk[:, 320:], w, preferred_element_type=jnp.float32)
+        for a in range(2):
+            acc[a] += lax.dot_general(xbuf[k, a], w, (((0,), (0,)), ((), ())), preferred_element_type=jnp.float32)
         return carry
 
     lax.fori_loop(0, 16, first, 0)
@@ -311,30 +353,37 @@
             out_p[cc * 8 + zz] = src[0]
             out_t[cc * 8 + zz] = src[1]
 
-    @pl.when(jnp.logical_not(stays))
+    @pl.when(moves)
     def _():
-        for i, (src, _dst, away) in enumerate(pieces):
-            copy(src, away, swap_s.at[i], swap_r.at[i], partner).wait_send()
+        for i in range(6):
+            swap_copy(i).wait_send()
+
+    for e in range(2):
+        @pl.when(passes[e])
+        def _():
+            for i in (0, 2, 4):
+                relay_copy(i + e).wait_send()
 
     for c in sends:
         c.wait_send()
 
 
 def shards(primal, tangent, w_in, b_in, w_out, b_out, gate_mod, gate_tan):
-    x_in = jnp.concatenate([primal, tangent], 1)
-    w = jnp.stack([w_in, w_out.T])
-    gates = jnp.stack([b_out, gate_mod, gate_tan]).reshape(3, 16, 320).transpose(1, 0, 2)
+    tables = [t.reshape(40, 128) for t in (b_out, gate_mod, gate_tan)]
     bf, dma = jnp.bfloat16, pltpu.SemaphoreType.DMA
     both = lambda *shape: [dma(shape), dma(shape)]
     return pl.pallas_call(
         kernel,
         out_shape=[jax.ShapeDtypeStruct((16, 16, 320), bf)] * 2,
-        in_specs=[pl.BlockSpec(memory_space=pltpu.VMEM)] * 4,
+        in_specs=[pl.BlockSpec(memory_space=pltpu.VMEM)] * 8,
         out_specs=[pl.BlockSpec(memory_space=pltpu.VMEM)] * 2,
         scratch_shapes=[
             pltpu.VMEM((2, 8, 2, 320, 864), bf),
-            pltpu.VMEM((16, 256, 640), bf),
+            pltpu.VMEM((16, 2, 320, 256), bf),
+            pltpu.VMEM((2, 160, 864), bf),
+            pltpu.VMEM((320, 256), bf),
             pltpu.VMEM((2, 1, 864), jnp.float32),
+            pltpu.VMEM((16, 3, 320), jnp.float32),
             pltpu.VMEM((2, 256, 864), jnp.float32),
             pltpu.VMEM((2, 2, 128, 864), bf),
             pltpu.VMEM((8, 2, 2, 2, 4, 16, 640), bf),
@@ -346,15 +395,15 @@
             pltpu.VMEM((8, 3, 16, 640), bf),
             pltpu.VMEM((8, 2, 2, 16, 320), bf),
             pltpu.VMEM((8, 2, 2, 16, 320), bf),
-            *both(6), dma, dma, *both(2, 2, 2, 4), *both(2, 2, 8),
-            *both(2, 3), *both(2, 4, 3), *both(8, 2, 3), *both(8, 2, 3), *both(8, 2),
+            *both(6), *both(6), dma, dma, *both(2, 2, 2, 4), *both(2, 2, 8),
+            *both(2, 8, 2), *both(2, 8, 2), *both(8, 2, 3), *both(8, 2, 3), *both(8, 2),
         ],
         compiler_params=pltpu.CompilerParams(
             collective_id=0, has_side_effects=True, vmem_limit_bytes=56 << 20
         ),
         cost_estimate=pl.CostEstimate(flops=9 * 10**9, bytes_accessed=3 * 10**6, transcendentals=221184),
         name="ffn_pair",
-    )(x_in, w, b_in.reshape(1, 864), gates)
+    )(primal.T, tangent.T, w_in, w_out.T, b_in, *tables)
 
 
 def solution(mesh):

time: 167 us -> 152 us (0.910)
  local copies, waits for them, and re-layouts: 9.21 us -> 2.34 us
  Pallas kernels: 154 us -> 148 us
  other arithmetic: 2.74 us -> 0 us
    pallas_call x1, Pallas kernels: 154 us -> 148 us  [shards(): pl.pallas_call(kernel, out_shape=[jax.ShapeDtypeStruct((16, 16, 320), bf)...]
    unnamed x8 -> x4, local copies, waits for them, and re-layouts: 5.41 us -> 2.34 us
    another operation x3 -> x0, local copies, waits for them, and re-layouts: 2.44 us -> none  [shards(): jnp.stack([b_out, gate_mod, gate_tan]).reshape(3, 16, 320)]
where the time goes in v2:
time: 152 us; the launch traced here: 151 us
  Pallas kernels  148 us (97%)
  local copies, waits for them, and re-layouts  2.34 us (2%)
    pallas_call x1, Pallas kernels, shards(): pl.pallas_call(kernel, out_shape=[jax.ShapeDtypeStruct((16, 16, 320), bf)...  148 us

profile of v2, /device:TPU:1, one launch (start us, length us, event | category | flops | bytes accessed | tf_op | source)
XLA Modules:
  0.0 151.5 jit_solution(6017559079937862158)
XLA Ops:
  0.6 148.5 %ffn_pair.1 = (bf16[16,16,320]{2,1,0:T(8,128)(2,1)}, bf16[16,16,320]{2,1,0:T(8,128)(2,1)}) custom-call(bf16[320,256]{1,0:T(8,128)(2,1)} %bitcast.7, bf16[320,256]{1,0:T(8,128)(2,1)} %bitcast.8, bf16[320,864]{1,0:T(8,128)(2,1)} %w_in.1, bf16[320,864]{1,0:T(8,128)(2,1)} %bitcast.6, f32[864]{0:T(1024)} %b_in.1, f32[40,128]{1,0:T(8,128)} %bitcast.9, ...), custom_call_target="tpu_custom_call" | custom-call | flops 8999999488 | bytes 3000000 | tf_op jit(solution)/shard_map/ffn_pair/pallas_call | solution.py:375
  149.1 0.0 copy-start
  149.1 1.7 %copy.12 = bf16[16,16,320]{2,1,0:T(8,128)(2,1)} copy(bf16[16,16,320]{2,1,0:T(8,128)(2,1)} %get-tuple-element.4) | data formatting | bytes 327680
  150.8 0.0 copy-done
  150.8 0.7 copy.13
Async XLA Ops:
  149.1 1.7 %copy-start = (bf16[16,16,320]{2,1,0:T(8,128)(2,1)S(1)}, bf16[16,16,320]{2,1,0:T(8,128)(2,1)}, u32[]{:S(2)}) copy-start(bf16[16,16,320]{2,1,0:T(8,128)(2,1)} %get-tuple-element.5) | copy-start | bytes 491524

commit v3 on v2

--- a/solution.py
+++ b/solution.py
@@ -32,9 +32,9 @@
     xp_in, xt_in, w_in, w_out, b_in, b_out, gate_mod, gate_tan,
     out_p, out_t,
     wbuf, xbuf, relay_w, relay_x, bias, gates, acc, hid,
-    part, r1x, r1y, s2x, s2y, r2x, r2y, fin, land,
+    part, r0, r1, s2, r2, fin, land,
     swap_s, swap_r, relay_s, relay_r, bias_s, bias_r, ring_s, ring_r, sib_s, sib_r,
-    xs_s, xs_r, xf_s, xf_r, rs1_s, rs1_r, rs2_s, rs2_r, fin_s, fin_r,
+    xs_s, xs_r, xf_s, xf_r, rs0_s, rs0_r, rs1_s, rs1_r, rs2_s, rs2_r, fin_s, fin_r,
 ):
     f = lax.axis_index("fsdp")
     s = lax.axis_index("seq")
@@ -60,10 +60,11 @@
             src_ref=src, dst_ref=dst, send_sem=ssem, recv_sem=rsem, device_id=where, device_id_type=MESH
         )
 
-    def send(src, dst, ssem, rsem, where):
-        c = copy(src, dst, ssem, rsem, where)
-        c.start()
-        sends.append(c)
+    def send(src, dst, ssem, rsem, where, mode="start, note"):
+        if "start" in mode:
+            copy(src, dst, ssem, rsem, where).start()
+        if "note" in mode:
+            sends.append((src, dst, ssem, rsem, where))
 
     def arrived(dst, ssem, rsem, where):
         copy(dst, dst, ssem, rsem, where).wait_recv()
@@ -120,14 +121,14 @@
     def w_at(h, delta, q, who=None):
         return wbuf.at[h, delta % 8, core if who is None else who, rows(q)]
 
-    def ring_send(h, q, way, d):
+    def ring_send(h, q, way, d, mode="start, note"):
         send(
             w_at(h, -way * (d - 1), q), w_at(h, -way * d, q),
-            ring_s.at[h, q, (way + 1) // 2, d - 1], ring_r.at[h, q, (way + 1) // 2, d - 1], at(dz=way),
+            ring_s.at[h, q, (way + 1) // 2, d - 1], ring_r.at[h, q, (way + 1) // 2, d - 1], at(dz=way), mode,
         )
 
-    def sib_send(h, q, delta):
-        send(w_at(h, delta, q), w_at(h, delta, q), sib_s.at[h, q, delta % 8], sib_r.at[h, q, delta % 8], at(flip=True))
+    def sib_send(h, q, delta, mode="start, note"):
+        send(w_at(h, delta, q), w_at(h, delta, q), sib_s.at[h, q, delta % 8], sib_r.at[h, q, delta % 8], at(flip=True), mode)
 
     def sib_wait(h, delta):
         for q in range(2):
@@ -146,10 +147,10 @@
                     ring_send(h, q, way, d + 1)
                 sib_send(h, q, -way * d)
 
-    def ring_open(h, q):
+    def ring_open(h, q, mode="start, note"):
         for way in (1, -1):
-            ring_send(h, q, way, 1)
-        sib_send(h, q, 0)
+            ring_send(h, q, way, 1, mode)
+        sib_send(h, q, 0, mode)
 
     def slot(a, o1, o2, part_of=None):
         dx, dy = (o1, o2) if a == 0 else (o2, o1)
@@ -163,11 +164,11 @@
     def offset(stage, r, d):
         return (d, 0) if stage == 0 else (OFF[r], d)
 
-    def bc_open(a, stage, r=0):
+    def bc_open(a, stage, r=0, mode="start, note"):
         for wi, way in enumerate((1, -1)):
             src = slot(a, *offset(stage, r, 0))
             i = stage * 4 + r
-            send(src, src, xs_s.at[a, i, wi], xs_r.at[a, i, wi], along(a, stage, way))
+            send(src, src, xs_s.at[a, i, wi], xs_r.at[a, i, wi], along(a, stage, way), mode)
 
     def bc_pass(a, stage, r=0):
         for wi, way in enumerate((1, -1)):
@@ -186,15 +187,39 @@
         swap_open(i)
     bias[core] = b_in[...].reshape(1, 864)
     send(bias.at[core], bias.at[core], bias_s, bias_r, at(flip=True))
+
+    def open_w(mode):
+        for q in range(2):
+            if mode == "start":
+                own(q)
+            ring_open(0, q, mode)
+
+    def open_x(mode):
+        for a in range(2):
+            if mode == "start":
+                own(2 + a)
+            bc_open(a, 0, 0, mode)
+            bc_open(a, 1, 0, mode)
+
+    @pl.when(stays)
+    def _():
+        open_w("start")
+        open_x("start")
+
     swap_pass(0)
-    for q in range(2):
-        own(q)
-        ring_open(0, q)
+
+    @pl.when(moves)
+    def _():
+        open_w("start")
+
     swap_pass(2)
-    for a in range(2):
-        own(2 + a)
-        bc_open(a, 0)
-        bc_open(a, 1, 0)
+
+    @pl.when(moves)
+    def _():
+        open_x("start")
+
+    open_w("note")
+    open_x("note")
     acc[...] = jnp.zeros_like(acc)
     for n, table in enumerate((b_out, gate_mod, gate_tan)):
         for i in range(16):
@@ -227,20 +252,23 @@
     for r in range(4):
         for a in range(2):
             bc_end(a, 1, r)
-    ring_step(0, 4)
-    for delta in ORDER:
-        sib_wait(0, delta)
-    arrived(bias.at[1 - core], bias_s, bias_r, at(flip=True))
 
     def first(i, carry):
-        delta, h = i // 2, lax.rem(i, 2)
+        delta, h = lax.rem(i // 2 + 6, 8), lax.rem(i, 2)
         k = h * 8 + lax.rem(z + delta, 8)
         w = wbuf[0, delta, h]
         for a in range(2):
             acc[a] += lax.dot_general(xbuf[k, a], w, (((0,), (0,)), ((), ())), preferred_element_type=jnp.float32)
         return carry
 
-    lax.fori_loop(0, 16, first, 0)
+    for delta in ORDER[:5]:
+        sib_wait(0, delta)
+    lax.fori_loop(0, 10, first, 0)
+    ring_step(0, 4)
+    for delta in ORDER[5:]:
+        sib_wait(0, delta)
+    lax.fori_loop(10, 16, first, 0)
+    arrived(bias.at[1 - core], bias_s, bias_r, at(flip=True))
 
     def activate(i, carry):
         r = pl.ds(pl.multiple_of(i * 32, 32), 32)
@@ -262,57 +290,57 @@
                 preferred_element_type=jnp.float32,
             )
             packed = jnp.concatenate([both[:128], both[128:]], axis=1).astype(jnp.bfloat16)
-            for b in range(8):
-                part[i, b % 2, h, yl, b // 2] = packed[b * 16 : (b + 1) * 16]
+            for b in range(4):
+                part[i, 0, b, j] = packed[b * 32 : b * 32 + 16]
+                part[i, 1, j, b] = packed[b * 32 + 16 : b * 32 + 32]
             return carry
 
         lax.fori_loop(0, 4, body, 0)
-        for d in (1, 2, 3):
-            xx = lax.rem(x + d, 4)
-            send(part.at[i, 0, :, :, xx], r1x.at[i, d - 1], rs1_s.at[i, 0, d - 1], rs1_r.at[i, 0, d - 1], at(dx=d))
-            yy = lax.rem(y + d, 4)
-            send(
-                part.at[i, 1, yy // 2, lax.rem(yy, 2)], r1y.at[i, d - 1],
-                rs1_s.at[i, 1, d - 1], rs1_r.at[i, 1, d - 1], at(dy=d),
-            )
+        for a in range(2):
+            for wi, way in enumerate((1, -1)):
+                send(
+                    part.at[i, a, there(a, 2), pl.ds(2 * wi, 2)], r0.at[i, a, wi],
+                    rs0_s.at[i, a, wi], rs0_r.at[i, a, wi], along(a, 0, way),
+                )
 
     f32 = lambda v: v.astype(jnp.float32)
 
+    def there(a, d):
+        return lax.rem((x if a == 0 else y) + d + 4, 4)
+
+    def reduce_zero(i):
+        for a in range(2):
+            for wi, way in enumerate((1, -1)):
+                arrived(r0.at[i, a, wi], rs0_s.at[i, a, wi], rs0_r.at[i, a, wi], along(a, 0, way))
+                j = there(a, way)
+                for b in range(2):
+                    t = f32(part[i, a, j, 2 * wi + b]) + f32(r0[i, a, wi, b])
+                    part[i, a, j, 2 * wi + b] = t.astype(jnp.bfloat16)
+                send(part.at[i, a, j], r1.at[i, a, wi], rs1_s.at[i, a, wi], rs1_r.at[i, a, wi], along(a, 0, way))
+
     def reduce_one(i):
-        for d in (1, 2, 3):
-            arrived(r1x.at[i, d - 1], rs1_s.at[i, 0, d - 1], rs1_r.at[i, 0, d - 1], at(dx=-d))
-        for h in range(2):
-            for yl in range(2):
-                t = f32(part[i, 0, h, yl, x])
-                for d in range(3):
-                    t += f32(r1x[i, d, h, yl])
-                s2x[i, h, yl] = t.astype(jnp.bfloat16)
-        for d in (1, 2, 3):
-            yy = lax.rem(y + d, 4)
-            send(
-                s2x.at[i, yy // 2, lax.rem(yy, 2)], r2x.at[i, d - 1],
-                rs2_s.at[i, 0, d - 1], rs2_r.at[i, 0, d - 1], at(dy=d),
-            )
-        for d in (1, 2, 3):
-            arrived(r1y.at[i, d - 1], rs1_s.at[i, 1, d - 1], rs1_r.at[i, 1, d - 1], at(dy=-d))
-        for b in range(4):
-            t = f32(part[i, 1, y_hi, y_lo, b])
-            for d in range(3):
-                t += f32(r1y[i, d, b])
-            s2y[i, b] = t.astype(jnp.bfloat16)
-        for d in (1, 2, 3):
-            send(s2y.at[i, lax.rem(x + d, 4)], r2y.at[i, d - 1], rs2_s.at[i, 1, d - 1], rs2_r.at[i, 1, d - 1], at(dx=d))
+        for a in range(2):
+            for wi, way in enumerate((1, -1)):
+                arrived(r1.at[i, a, wi], rs1_s.at[i, a, wi], rs1_r.at[i, a, wi], along(a, 0, way))
+            for b in range(4):
+                t = f32(part[i, a, there(a, 0), b]) + f32(r1[i, a, 0, b]) + f32(r1[i, a, 1, b])
+                s2[i, a, b] = t.astype(jnp.bfloat16)
+            for d in (1, 2, 3):
+                send(
+                    s2.at[i, a, there(1 - a, d)], r2.at[i, a, d - 1],
+                    rs2_s.at[i, a, d - 1], rs2_r.at[i, a, d - 1], along(a, 1, d),
+                )
 
     def reduce_two(i):
         delta = ORDER[i]
         g = gates[y_hi * 8 + lax.rem(z + delta, 8)]
         for d in (1, 2, 3):
-            arrived(r2x.at[i, d - 1], rs2_s.at[i, 0, d - 1], rs2_r.at[i, 0, d - 1], at(dy=-d))
-            arrived(r2y.at[i, d - 1], rs2_s.at[i, 1, d - 1], rs2_r.at[i, 1, d - 1], at(dx=-d))
+            for a in range(2):
+                arrived(r2.at[i, a, d - 1], rs2_s.at[i, a, d - 1], rs2_r.at[i, a, d - 1], along(a, 1, d))
         for cc in range(2):
-            t = f32(s2x[i, y_hi, y_lo]) if cc == 0 else f32(s2y[i, x])
+            t = f32(s2[i, cc, there(1 - cc, 0)])
             for d in range(3):
-                t += f32((r2x, r2y)[cc][i, d])
+                t += f32(r2[i, cc, d])
             shifted = t[:, :320] + g[0:1]
             fin[i, cc, 0] = (g[1:2] * shifted).astype(jnp.bfloat16)
             fin[i, cc, 1] = (g[1:2] * t[:, 320:] + g[2:3] * shifted).astype(jnp.bfloat16)
@@ -320,25 +348,36 @@
             send(fin.at[i, core], land.at[i, 0], fin_s.at[i, 0], fin_r.at[i, 0], at(dz=delta))
         send(fin.at[i, 1 - core], land.at[i, 1], fin_s.at[i, 1], fin_r.at[i, 1], at(dz=delta, flip=True))
 
-    groups = ((0,), (1, 2), (3, 4), (5, 6), (7,))
-    for d in range(5):
+    def each(what, *items):
+        for i in items:
+            what(i)
+
+    def blocks(d, *items):
         if d:
             ring_step(1, d)
-        for i in groups[d]:
+        for i in items:
             sib_wait(1, ORDER[i])
             second(i)
-        if d >= 1:
-            for i in groups[d - 1]:
-                reduce_one(i)
-        if d >= 2:
-            for i in groups[d - 2]:
-                reduce_two(i)
-    for i in groups[3]:
-        reduce_two(i)
-    for i in groups[4]:
-        reduce_one(i)
-    for i in groups[4]:
-        reduce_two(i)
+
+    blocks(0, 0)
+    blocks(1, 1, 2)
+    each(reduce_zero, 0)
+    each(reduce_one, 0)
+    each(reduce_zero, 1, 2)
+    each(reduce_one, 1, 2)
+    blocks(2, 3, 4)
+    each(reduce_two, 0, 1, 2)
+    each(reduce_zero, 3, 4)
+    each(reduce_one, 3, 4)
+    blocks(3, 5, 6)
+    each(reduce_two, 3, 4)
+    each(reduce_zero, 5, 6)
+    blocks(4, 7)
+    each(reduce_one, 5, 6)
+    each(reduce_zero, 7)
+    each(reduce_two, 5, 6)
+    each(reduce_one, 7)
+    each(reduce_two, 7)
 
     for i in range(8):
         delta = ORDER[i]
@@ -365,7 +404,7 @@
                 relay_copy(i + e).wait_send()
 
     for c in sends:
-        c.wait_send()
+        copy(*c).wait_send()
 
 
 def shards(primal, tangent, w_in, b_in, w_out, b_out, gate_mod, gate_tan):
@@ -386,17 +425,15 @@
             pltpu.VMEM((16, 3, 320), jnp.float32),
             pltpu.VMEM((2, 256, 864), jnp.float32),
             pltpu.VMEM((2, 2, 128, 864), bf),
-            pltpu.VMEM((8, 2, 2, 2, 4, 16, 640), bf),
-            pltpu.VMEM((8, 3, 2, 2, 16, 640), bf),
-            pltpu.VMEM((8, 3, 4, 16, 640), bf),
-            pltpu.VMEM((8, 2, 2, 16, 640), bf),
-            pltpu.VMEM((8, 4, 16, 640), bf),
-            pltpu.VMEM((8, 3, 16, 640), bf),
-            pltpu.VMEM((8, 3, 16, 640), bf),
+            pltpu.VMEM((8, 2, 4, 4, 16, 640), bf),
+            pltpu.VMEM((8, 2, 2, 2, 16, 640), bf),
+            pltpu.VMEM((8, 2, 2, 4, 16, 640), bf),
+            pltpu.VMEM((8, 2, 4, 16, 640), bf),
+            pltpu.VMEM((8, 2, 3, 16, 640), bf),
             pltpu.VMEM((8, 2, 2, 16, 320), bf),
             pltpu.VMEM((8, 2, 2, 16, 320), bf),
             *both(6), *both(6), dma, dma, *both(2, 2, 2, 4), *both(2, 2, 8),
-            *both(2, 8, 2), *both(2, 8, 2), *both(8, 2, 3), *both(8, 2, 3), *both(8, 2),
+            *both(2, 8, 2), *both(2, 8, 2), *both(8, 2, 2), *both(8, 2, 2), *both(8, 2, 3), *both(8, 2),
         ],
         compiler_params=pltpu.CompilerParams(
             collective_id=0, has_side_effects=True, vmem_limit_bytes=56 << 20

time: 152 us -> 154 us (1.013)
  Pallas kernels: 148 us -> 151 us
    pallas_call x1, Pallas kernels: 148 us -> 151 us  [shards(): pl.pallas_call(kernel, out_shape=[jax.ShapeDtypeStruct((16, 16, 320), bf)...]
where the time goes in v3:
time: 154 us; the launch traced here: 153 us
  Pallas kernels  151 us (98%)
  local copies, waits for them, and re-layouts  2.34 us (2%)
    pallas_call x1, Pallas kernels, shards(): pl.pallas_call(kernel, out_shape=[jax.ShapeDtypeStruct((16, 16, 320), bf)...  151 us

profile of v3, /device:TPU:1, one launch (start us, length us, event | category | flops | bytes accessed | tf_op | source)
XLA Modules:
  0.0 153.5 jit_solution(16062939368228558385)
XLA Ops:
  0.6 150.5 %ffn_pair.1 = (bf16[16,16,320]{2,1,0:T(8,128)(2,1)}, bf16[16,16,320]{2,1,0:T(8,128)(2,1)}) custom-call(bf16[320,256]{1,0:T(8,128)(2,1)} %bitcast.7, bf16[320,256]{1,0:T(8,128)(2,1)} %bitcast.8, bf16[320,864]{1,0:T(8,128)(2,1)} %w_in.1, bf16[320,864]{1,0:T(8,128)(2,1)} %bitcast.6, f32[864]{0:T(1024)} %b_in.1, f32[40,128]{1,0:T(8,128)} %bitcast.9, ...), custom_call_target="tpu_custom_call" | custom-call | flops 8999999488 | bytes 3000000 | tf_op jit(solution)/shard_map/ffn_pair/pallas_call | solution.py:414
  151.1 0.0 copy-start
  151.2 1.7 %copy.12 = bf16[16,16,320]{2,1,0:T(8,128)(2,1)} copy(bf16[16,16,320]{2,1,0:T(8,128)(2,1)} %get-tuple-element.4) | data formatting | bytes 327680
  152.8 0.0 copy-done
  152.8 0.7 copy.13
Async XLA Ops:
  151.1 1.7 %copy-start = (bf16[16,16,320]{2,1,0:T(8,128)(2,1)S(1)}, bf16[16,16,320]{2,1,0:T(8,128)(2,1)}, u32[]{:S(2)}) copy-start(bf16[16,16,320]{2,1,0:T(8,128)(2,1)} %get-tuple-element.5) | copy-start | bytes 491524

commit v4 on v3

--- a/solution.py
+++ b/solution.py
@@ -60,14 +60,17 @@
             src_ref=src, dst_ref=dst, send_sem=ssem, recv_sem=rsem, device_id=where, device_id_type=MESH
         )
 
-    def send(src, dst, ssem, rsem, where, mode="start, note"):
-        if "start" in mode:
+    mode = ["start, note"]
+
+    def send(src, dst, ssem, rsem, where):
+        if "start" in mode[0]:
             copy(src, dst, ssem, rsem, where).start()
-        if "note" in mode:
+        if "note" in mode[0]:
             sends.append((src, dst, ssem, rsem, where))
 
     def arrived(dst, ssem, rsem, where):
-        copy(dst, dst, ssem, rsem, where).wait_recv()
+        if "start" in mode[0]:
+            copy(dst, dst, ssem, rsem, where).wait_recv()
 
     barrier = pltpu.get_barrier_semaphore()
     friends = [at(dz=d, flip=fl) for d in range(8) for fl in (False, True) if d or fl]
@@ -80,10 +83,9 @@
     rows = lambda q: pl.ds(q * 160, 160)
     stays = y_hi == core
     moves = jnp.logical_not(stays)
-    own_k = (y_lo * 4 + x) * 2 + y_hi
     sources = [w_in.at[rows(0)], w_in.at[rows(1)], xp_in, xt_in, w_out.at[rows(0)], w_out.at[rows(1)]]
     homes = [
-        wbuf.at[0, 0, core, rows(0)], wbuf.at[0, 0, core, rows(1)], xbuf.at[own_k, 0], xbuf.at[own_k, 1],
+        wbuf.at[0, 0, core, rows(0)], wbuf.at[0, 0, core, rows(1)], xbuf.at[x * 2 + y_hi, 0, y_lo], xbuf.at[x * 2 + y_hi, 1, y_lo],
         wbuf.at[1, 0, core, rows(0)], wbuf.at[1, 0, core, rows(1)],
     ]
     relays = [relay_w.at[0], relay_w.at[0], relay_x, relay_x, relay_w.at[1], relay_w.at[1]]
@@ -95,8 +97,7 @@
 
     def relay_copy(i):
         yy = lax.rem(y + step_of(i) + 4, 4)
-        k = (lax.rem(yy, 2) * 4 + x) * 2 + yy // 2
-        dst = xbuf.at[k, i % 2] if i in (2, 3) else homes[i]
+        dst = xbuf.at[x * 2 + yy // 2, i % 2, lax.rem(yy, 2)] if i in (2, 3) else homes[i]
         return copy(relays[i], dst, relay_s.at[i], relay_r.at[i], at(dy=step_of(i)))
 
     def swap_open(i):
@@ -121,14 +122,14 @@
     def w_at(h, delta, q, who=None):
         return wbuf.at[h, delta % 8, core if who is None else who, rows(q)]
 
-    def ring_send(h, q, way, d, mode="start, note"):
+    def ring_send(h, q, way, d):
         send(
             w_at(h, -way * (d - 1), q), w_at(h, -way * d, q),
-            ring_s.at[h, q, (way + 1) // 2, d - 1], ring_r.at[h, q, (way + 1) // 2, d - 1], at(dz=way), mode,
+            ring_s.at[h, q, (way + 1) // 2, d - 1], ring_r.at[h, q, (way + 1) // 2, d - 1], at(dz=way),
         )
 
-    def sib_send(h, q, delta, mode="start, note"):
-        send(w_at(h, delta, q), w_at(h, delta, q), sib_s.at[h, q, delta % 8], sib_r.at[h, q, delta % 8], at(flip=True), mode)
+    def sib_send(h, q, delta):
+        send(w_at(h, delta, q), w_at(h, delta, q), sib_s.at[h, q, delta % 8], sib_r.at[h, q, delta % 8], at(flip=True))
 
     def sib_wait(h, delta):
         for q in range(2):
@@ -147,16 +148,16 @@
                     ring_send(h, q, way, d + 1)
                 sib_send(h, q, -way * d)
 
-    def ring_open(h, q, mode="start, note"):
+    def ring_open(h, q):
         for way in (1, -1):
-            ring_send(h, q, way, 1, mode)
-        sib_send(h, q, 0, mode)
+            ring_send(h, q, way, 1)
+        sib_send(h, q, 0)
 
     def slot(a, o1, o2, part_of=None):
         dx, dy = (o1, o2) if a == 0 else (o2, o1)
         xx, yy = lax.rem(x + dx + 4, 4), lax.rem(y + dy + 4, 4)
-        k = (lax.rem(yy, 2) * 4 + xx) * 2 + yy // 2
-        return xbuf.at[k, a] if part_of is None else xbuf.at[k, a, rows(part_of)]
+        whole = (xx * 2 + yy // 2, a, lax.rem(yy, 2))
+        return xbuf.at[whole] if part_of is None else xbuf.at[(*whole, rows(part_of))]
 
     def along(a, stage, d):
         return at(dx=d) if (a == 0) == (stage == 0) else at(dy=d)
@@ -164,11 +165,11 @@
     def offset(stage, r, d):
         return (d, 0) if stage == 0 else (OFF[r], d)
 
-    def bc_open(a, stage, r=0, mode="start, note"):
+    def bc_open(a, stage, r=0):
         for wi, way in enumerate((1, -1)):
             src = slot(a, *offset(stage, r, 0))
             i = stage * 4 + r
-            send(src, src, xs_s.at[a, i, wi], xs_r.at[a, i, wi], along(a, stage, way), mode)
+            send(src, src, xs_s.at[a, i, wi], xs_r.at[a, i, wi], along(a, stage, way))
 
     def bc_pass(a, stage, r=0):
         for wi, way in enumerate((1, -1)):
@@ -183,43 +184,56 @@
             i = stage * 4 + r
             arrived(slot(a, *offset(stage, r, 2), wi), xf_s.at[a, i, wi], xf_r.at[a, i, wi], along(a, stage, way))
 
-    for i in range(4):
+    def branch(when, what):
+        mode[0] = "start"
+        pl.when(when)(what)
+        mode[0] = "start, note"
+
+    def note(what):
+        mode[0] = "note"
+        what()
+        mode[0] = "start, note"
+
+    def open_w():
+        for q in range(2):
+            if "start" in mode[0]:
+                own(q)
+            ring_open(0, q)
+
+    def open_x():
+        for a in range(2):
+            bc_open(a, 0, 0)
+            bc_open(a, 1, 0)
+
+    def x_head():
+        for a in range(2):
+            bc_pass(a, 0)
+            for r in (1, 2):
+                bc_open(a, 1, r)
+        for a in range(2):
+            bc_pass(a, 1, 0)
+        for a in range(2):
+            bc_end(a, 0)
+            bc_open(a, 1, 3)
+
+    def x_tail():
+        for r in (1, 2):
+            for a in range(2):
+                bc_pass(a, 1, r)
+
+    for i in (2, 3, 0, 1):
         swap_open(i)
     bias[core] = b_in[...].reshape(1, 864)
     send(bias.at[core], bias.at[core], bias_s, bias_r, at(flip=True))
 
-    def open_w(mode):
-        for q in range(2):
-            if mode == "start":
-                own(q)
-            ring_open(0, q, mode)
-
-    def open_x(mode):
-        for a in range(2):
-            if mode == "start":
-                own(2 + a)
-            bc_open(a, 0, 0, mode)
-            bc_open(a, 1, 0, mode)
-
-    @pl.when(stays)
-    def _():
-        open_w("start")
-        open_x("start")
-
+    branch(stays, open_w)
+    swap_pass(2)
     swap_pass(0)
-
-    @pl.when(moves)
-    def _():
-        open_w("start")
-
-    swap_pass(2)
-
-    @pl.when(moves)
-    def _():
-        open_x("start")
-
-    open_w("note")
-    open_x("note")
+    for a in range(2):
+        own(2 + a)
+    open_x()
+    branch(moves, open_w)
+    note(open_w)
     acc[...] = jnp.zeros_like(acc)
     for n, table in enumerate((b_out, gate_mod, gate_tan)):
         for i in range(16):
@@ -227,24 +241,14 @@
             flat = jnp.concatenate([table[first_row + j : first_row + j + 1, :] for j in range(3)], axis=1)
             gates[i, n : n + 1] = flat[:, lane : lane + 320]
     ring_step(0, 1)
-    for a in range(2):
-        bc_pass(a, 0)
-        for r in (1, 2):
-            bc_open(a, 1, r)
-    for a in range(2):
-        bc_pass(a, 1, 0)
-    for a in range(2):
-        bc_end(a, 0)
-        bc_open(a, 1, 3)
+    x_head()
+    ring_step(0, 2)
+    x_tail()
     for i in (4, 5):
         swap_open(i)
-    ring_step(0, 2)
-    for r in (1, 2):
-        for a in range(2):
-            bc_pass(a, 1, r)
-    swap_pass(4)
     for a in range(2):
         bc_pass(a, 1, 3)
+    swap_pass(4)
     ring_step(0, 3)
     for q in range(2):
         own(4 + q)
@@ -254,20 +258,20 @@
             bc_end(a, 1, r)
 
     def first(i, carry):
-        delta, h = lax.rem(i // 2 + 6, 8), lax.rem(i, 2)
-        k = h * 8 + lax.rem(z + delta, 8)
-        w = wbuf[0, delta, h]
-        for a in range(2):
-            acc[a] += lax.dot_general(xbuf[k, a], w, (((0,), (0,)), ((), ())), preferred_element_type=jnp.float32)
+        delta = lax.rem(i + 6, 8)
+        w = wbuf[0, delta].reshape(640, 864)
+        for a in range(2):
+            xk = xbuf[lax.rem(z + delta, 8), a].reshape(640, 256)
+            acc[a] += lax.dot_general(xk, w, (((0,), (0,)), ((), ())), preferred_element_type=jnp.float32)
         return carry
 
     for delta in ORDER[:5]:
         sib_wait(0, delta)
-    lax.fori_loop(0, 10, first, 0)
+    lax.fori_loop(0, 5, first, 0)
     ring_step(0, 4)
     for delta in ORDER[5:]:
         sib_wait(0, delta)
-    lax.fori_loop(10, 16, first, 0)
+    lax.fori_loop(5, 8, first, 0)
     arrived(bias.at[1 - core], bias_s, bias_r, at(flip=True))
 
     def activate(i, carry):
@@ -283,19 +287,21 @@
     def second(i):
         delta = ORDER[i]
 
-        def body(j, carry):
-            h, yl = j // 2, lax.rem(j, 2)
+        def body(h, carry):
             both = lax.dot_general(
-                hid[yl].reshape(256, 864), wbuf[1, delta, h], (((1,), (1,)), ((), ())),
+                hid[...].reshape(512, 864), wbuf[1, delta, h], (((1,), (1,)), ((), ())),
                 preferred_element_type=jnp.float32,
             )
-            packed = jnp.concatenate([both[:128], both[128:]], axis=1).astype(jnp.bfloat16)
-            for b in range(4):
-                part[i, 0, b, j] = packed[b * 32 : b * 32 + 16]
-                part[i, 1, j, b] = packed[b * 32 + 16 : b * 32 + 32]
+            for yl in range(2):
+                packed = jnp.concatenate(
+                    [both[yl * 256 : yl * 256 + 128], both[yl * 256 + 128 : yl * 256 + 256]], axis=1
+                ).astype(jnp.bfloat16)
+                for b in range(4):
+                    part[i, 0, b, h * 2 + yl] = packed[b * 32 : b * 32 + 16]
+                    part[i, 1, h * 2 + yl, b] = packed[b * 32 + 16 : b * 32 + 32]
             return carry
 
-        lax.fori_loop(0, 4, body, 0)
+        lax.fori_loop(0, 2, body, 0)
         for a in range(2):
             for wi, way in enumerate((1, -1)):
                 send(
@@ -361,21 +367,20 @@
 
     blocks(0, 0)
     blocks(1, 1, 2)
-    each(reduce_zero, 0)
+    each(reduce_zero, 0, 1, 2)
     each(reduce_one, 0)
-    each(reduce_zero, 1, 2)
+    blocks(2, 3, 4)
     each(reduce_one, 1, 2)
-    blocks(2, 3, 4)
-    each(reduce_two, 0, 1, 2)
     each(reduce_zero, 3, 4)
+    each(reduce_two, 0)
+    blocks(3, 5, 6)
     each(reduce_one, 3, 4)
-    blocks(3, 5, 6)
-    each(reduce_two, 3, 4)
     each(reduce_zero, 5, 6)
+    each(reduce_two, 1, 2)
     blocks(4, 7)
     each(reduce_one, 5, 6)
     each(reduce_zero, 7)
-    each(reduce_two, 5, 6)
+    each(reduce_two, 3, 4, 5, 6)
     each(reduce_one, 7)
     each(reduce_two, 7)
 
@@ -418,7 +423,7 @@
         out_specs=[pl.BlockSpec(memory_space=pltpu.VMEM)] * 2,
         scratch_shapes=[
             pltpu.VMEM((2, 8, 2, 320, 864), bf),
-            pltpu.VMEM((16, 2, 320, 256), bf),
+            pltpu.VMEM((8, 2, 2, 320, 256), bf),
             pltpu.VMEM((2, 160, 864), bf),
             pltpu.VMEM((320, 256), bf),
             pltpu.VMEM((2, 1, 864), jnp.float32),

time: 154 us -> 143 us (0.929)
  Pallas kernels: 151 us -> 140 us
    pallas_call x1, Pallas kernels: 151 us -> 140 us  [shards(): pl.pallas_call(kernel, out_shape=[jax.ShapeDtypeStruct((16, 16, 320), bf)...]
where the time goes in v4:
time: 143 us
  Pallas kernels  140 us (98%)
  local copies, waits for them, and re-layouts  2.34 us (2%)
    pallas_call x1, Pallas kernels, shards(): pl.pallas_call(kernel, out_shape=[jax.ShapeDtypeStruct((16, 16, 320), bf)...  140 us

profile of v4, /device:TPU:1, one launch (start us, length us, event | category | flops | bytes accessed | tf_op | source)
XLA Modules:
  0.0 142.8 jit_solution(12140765831359345099)
XLA Ops:
  0.6 139.8 %ffn_pair.1 = (bf16[16,16,320]{2,1,0:T(8,128)(2,1)}, bf16[16,16,320]{2,1,0:T(8,128)(2,1)}) custom-call(bf16[320,256]{1,0:T(8,128)(2,1)} %bitcast.7, bf16[320,256]{1,0:T(8,128)(2,1)} %bitcast.8, bf16[320,864]{1,0:T(8,128)(2,1)} %w_in.1, bf16[320,864]{1,0:T(8,128)(2,1)} %bitcast.6, f32[864]{0:T(1024)} %b_in.1, f32[40,128]{1,0:T(8,128)} %bitcast.9, ...), custom_call_target="tpu_custom_call" | custom-call | flops 8999999488 | bytes 3000000 | tf_op jit(solution)/shard_map/ffn_pair/pallas_call | solution.py:419
  140.5 0.0 copy-start
  140.5 1.7 %copy.12 = bf16[16,16,320]{2,1,0:T(8,128)(2,1)} copy(bf16[16,16,320]{2,1,0:T(8,128)(2,1)} %get-tuple-element.4) | data formatting | bytes 327680
  142.1 0.0 copy-done
  142.1 0.7 copy.13
Async XLA Ops:
  140.5 1.7 %copy-start = (bf16[16,16,320]{2,1,0:T(8,128)(2,1)S(1)}, bf16[16,16,320]{2,1,0:T(8,128)(2,1)}, u32[]{:S(2)}) copy-start(bf16[16,16,320]{2,1,0:T(8,128)(2,1)} %get-tuple-element.5) | copy-start | bytes 491524

commit v5 on v4

--- a/solution.py
+++ b/solution.py
@@ -73,8 +73,8 @@
             copy(dst, dst, ssem, rsem, where).wait_recv()
 
     barrier = pltpu.get_barrier_semaphore()
-    friends = [at(dz=d, flip=fl) for d in range(8) for fl in (False, True) if d or fl]
-    friends += [at(dx=d) for d in (1, 2, 3)] + [at(dy=d) for d in (1, 2, 3)]
+    friends = [at(dz=d) for d in (1, 7)] + [at(flip=True)]
+    friends += [at(dx=d) for d in (1, 3)] + [at(dy=d) for d in (1, 3)]
     friends += [at(dy=d, flip=True) for d in (1, 3)]
     for who in friends:
         pl.semaphore_signal(barrier, inc=1, device_id=who, device_id_type=MESH)
@@ -83,12 +83,15 @@
     rows = lambda q: pl.ds(q * 160, 160)
     stays = y_hi == core
     moves = jnp.logical_not(stays)
-    sources = [w_in.at[rows(0)], w_in.at[rows(1)], xp_in, xt_in, w_out.at[rows(0)], w_out.at[rows(1)]]
+    eighty = lambda n: pl.ds(n * 80, 80)
+    sources = [w_in.at[eighty(0)], w_in.at[eighty(1)], xp_in, xt_in, w_out.at[rows(0)], w_out.at[rows(1)]]
+    sources += [w_in.at[eighty(2)], w_in.at[eighty(3)]]
     homes = [
-        wbuf.at[0, 0, core, rows(0)], wbuf.at[0, 0, core, rows(1)], xbuf.at[x * 2 + y_hi, 0, y_lo], xbuf.at[x * 2 + y_hi, 1, y_lo],
+        wbuf.at[0, 0, core, eighty(0)], wbuf.at[0, 0, core, eighty(1)], xbuf.at[x * 2 + y_hi, 0, y_lo], xbuf.at[x * 2 + y_hi, 1, y_lo],
         wbuf.at[1, 0, core, rows(0)], wbuf.at[1, 0, core, rows(1)],
+        wbuf.at[0, 0, core, eighty(2)], wbuf.at[0, 0, core, eighty(3)],
     ]
-    relays = [relay_w.at[0], relay_w.at[0], relay_x, relay_x, relay_w.at[1], relay_w.at[1]]
+    relays = [relay_w.at[0, eighty(0)]] * 2 + [relay_x] * 2 + [relay_w.at[1]] * 2 + [relay_w.at[0, eighty(1)]] * 2
     passes = [(lax.rem(y + (3 if e == 0 else 1), 4) // 2) == core for e in range(2)]
     step_of = lambda i: 1 if i % 2 == 0 else -1
 
@@ -197,7 +200,8 @@
     def open_w():
         for q in range(2):
             if "start" in mode[0]:
-                own(q)
+                own(6 * q)
+                own(6 * q + 1)
             ring_open(0, q)
 
     def open_x():
@@ -221,7 +225,7 @@
             for a in range(2):
                 bc_pass(a, 1, r)
 
-    for i in (2, 3, 0, 1):
+    for i in (2, 3, 0, 1, 6, 7):
         swap_open(i)
     bias[core] = b_in[...].reshape(1, 864)
     send(bias.at[core], bias.at[core], bias_s, bias_r, at(flip=True))
@@ -229,6 +233,7 @@
     branch(stays, open_w)
     swap_pass(2)
     swap_pass(0)
+    swap_pass(6)
     for a in range(2):
         own(2 + a)
     open_x()
@@ -272,6 +277,7 @@
     for delta in ORDER[5:]:
         sib_wait(0, delta)
     lax.fori_loop(5, 8, first, 0)
+    ring_step(1, 1)
     arrived(bias.at[1 - core], bias_s, bias_r, at(flip=True))
 
     def activate(i, carry):
@@ -358,31 +364,37 @@
         for i in items:
             what(i)
 
-    def blocks(d, *items):
-        if d:
-            ring_step(1, d)
-        for i in items:
-            sib_wait(1, ORDER[i])
-            second(i)
-
-    blocks(0, 0)
-    blocks(1, 1, 2)
-    each(reduce_zero, 0, 1, 2)
-    each(reduce_one, 0)
-    blocks(2, 3, 4)
-    each(reduce_one, 1, 2)
+    def block(i):
+        sib_wait(1, ORDER[i])
+        second(i)
+
+    block(0)
+    block(1)
+    reduce_zero(0)
+    block(2)
+    reduce_one(0)
+    each(reduce_zero, 1, 2)
+    ring_step(1, 2)
+    block(3)
+    reduce_one(1)
+    block(4)
+    reduce_one(2)
+    reduce_two(0)
     each(reduce_zero, 3, 4)
-    each(reduce_two, 0)
-    blocks(3, 5, 6)
-    each(reduce_one, 3, 4)
+    ring_step(1, 3)
+    block(5)
+    reduce_one(3)
+    block(6)
+    reduce_one(4)
+    each(reduce_two, 1, 2)
     each(reduce_zero, 5, 6)
-    each(reduce_two, 1, 2)
-    blocks(4, 7)
+    ring_step(1, 4)
+    block(7)
     each(reduce_one, 5, 6)
-    each(reduce_zero, 7)
+    reduce_zero(7)
     each(reduce_two, 3, 4, 5, 6)
-    each(reduce_one, 7)
-    each(reduce_two, 7)
+    reduce_one(7)
+    reduce_two(7)
 
     for i in range(8):
         delta = ORDER[i]
@@ -399,13 +411,13 @@
 
     @pl.when(moves)
     def _():
-        for i in range(6):
+        for i in range(8):
             swap_copy(i).wait_send()
 
     for e in range(2):
         @pl.when(passes[e])
         def _():
-            for i in (0, 2, 4):
+            for i in (0, 2, 4, 6):
                 relay_copy(i + e).wait_send()
 
     for c in sends:
@@ -437,7 +449,7 @@
             pltpu.VMEM((8, 2, 3, 16, 640), bf),
             pltpu.VMEM((8, 2, 2, 16, 320), bf),
             pltpu.VMEM((8, 2, 2, 16, 320), bf),
-            *both(6), *both(6), dma, dma, *both(2, 2, 2, 4), *both(2, 2, 8),
+            *both(8), *both(8), dma, dma, *both(2, 2, 2, 4), *both(2, 2, 8),
             *both(2, 8, 2), *both(2, 8, 2), *both(8, 2, 2), *both(8, 2, 2), *both(8, 2, 3), *both(8, 2),
         ],
         compiler_params=pltpu.CompilerParams(

time: 143 us -> 139 us (0.972)
  Pallas kernels: 140 us -> 136 us
    pallas_call x1, Pallas kernels: 140 us -> 136 us  [shards(): pl.pallas_call(kernel, out_shape=[jax.ShapeDtypeStruct((16, 16, 320), bf)...]
where the time goes in v5:
time: 139 us
  Pallas kernels  136 us (98%)
  local copies, waits for them, and re-layouts  2.34 us (2%)
    pallas_call x1, Pallas kernels, shards(): pl.pallas_call(kernel, out_shape=[jax.ShapeDtypeStruct((16, 16, 320), bf)...  136 us

profile of v5, /device:TPU:1, one launch (start us, length us, event | category | flops | bytes accessed | tf_op | source)
XLA Modules:
  0.0 138.6 jit_solution(6814042032857252181)
XLA Ops:
  0.6 135.6 %ffn_pair.1 = (bf16[16,16,320]{2,1,0:T(8,128)(2,1)}, bf16[16,16,320]{2,1,0:T(8,128)(2,1)}) custom-call(bf16[320,256]{1,0:T(8,128)(2,1)} %bitcast.7, bf16[320,256]{1,0:T(8,128)(2,1)} %bitcast.8, bf16[320,864]{1,0:T(8,128)(2,1)} %w_in.1, bf16[320,864]{1,0:T(8,128)(2,1)} %bitcast.6, f32[864]{0:T(1024)} %b_in.1, f32[40,128]{1,0:T(8,128)} %bitcast.9, ...), custom_call_target="tpu_custom_call" | custom-call | flops 8999999488 | bytes 3000000 | tf_op jit(solution)/shard_map/ffn_pair/pallas_call | solution.py:431
  136.2 0.0 copy-start
  136.3 1.7 %copy.12 = bf16[16,16,320]{2,1,0:T(8,128)(2,1)} copy(bf16[16,16,320]{2,1,0:T(8,128)(2,1)} %get-tuple-element.4) | data formatting | bytes 327680
  137.9 0.0 copy-done
  137.9 0.7 copy.13
Async XLA Ops:
  136.2 1.7 %copy-start = (bf16[16,16,320]{2,1,0:T(8,128)(2,1)S(1)}, bf16[16,16,320]{2,1,0:T(8,128)(2,1)}, u32[]{:S(2)}) copy-start(bf16[16,16,320]{2,1,0:T(8,128)(2,1)} %get-tuple-element.5) | copy-start | bytes 491524

commit v6 on v5

--- a/solution.py
+++ b/solution.py
@@ -30,7 +30,7 @@
 
 def kernel(
     xp_in, xt_in, w_in, w_out, b_in, b_out, gate_mod, gate_tan,
-    out_p, out_t,
+    out,
     wbuf, xbuf, relay_w, relay_x, bias, gates, acc, hid,
     part, r0, r1, s2, r2, fin, land,
     swap_s, swap_r, relay_s, relay_r, bias_s, bias_r, ring_s, ring_r, sib_s, sib_r,
@@ -337,7 +337,7 @@
             for b in range(4):
                 t = f32(part[i, a, there(a, 0), b]) + f32(r1[i, a, 0, b]) + f32(r1[i, a, 1, b])
                 s2[i, a, b] = t.astype(jnp.bfloat16)
-            for d in (1, 2, 3):
+            for d in (2, 1, 3):
                 send(
                     s2.at[i, a, there(1 - a, d)], r2.at[i, a, d - 1],
                     rs2_s.at[i, a, d - 1], rs2_r.at[i, a, d - 1], along(a, 1, d),
@@ -406,8 +406,8 @@
                 src = land[i, other]
             else:
                 src = fin[i, core]
-            out_p[cc * 8 + zz] = src[0]
-            out_t[cc * 8 + zz] = src[1]
+            out[0, cc * 8 + zz] = src[0]
+            out[1, cc * 8 + zz] = src[1]
 
     @pl.when(moves)
     def _():
@@ -424,15 +424,20 @@
         copy(*c).wait_send()
 
 
+def part_ways(both, out_p, out_t):
+    out_p[...] = both[0]
+    out_t[...] = both[1]
+
+
 def shards(primal, tangent, w_in, b_in, w_out, b_out, gate_mod, gate_tan):
     tables = [t.reshape(40, 128) for t in (b_out, gate_mod, gate_tan)]
     bf, dma = jnp.bfloat16, pltpu.SemaphoreType.DMA
     both = lambda *shape: [dma(shape), dma(shape)]
-    return pl.pallas_call(
+    both_out = pl.pallas_call(
         kernel,
-        out_shape=[jax.ShapeDtypeStruct((16, 16, 320), bf)] * 2,
+        out_shape=jax.ShapeDtypeStruct((2, 16, 16, 320), bf),
         in_specs=[pl.BlockSpec(memory_space=pltpu.VMEM)] * 8,
-        out_specs=[pl.BlockSpec(memory_space=pltpu.VMEM)] * 2,
+        out_specs=pl.BlockSpec(memory_space=pltpu.VMEM),
         scratch_shapes=[
             pltpu.VMEM((2, 8, 2, 320, 864), bf),
             pltpu.VMEM((8, 2, 2, 320, 256), bf),
@@ -458,6 +463,13 @@
         cost_estimate=pl.CostEstimate(flops=9 * 10**9, bytes_accessed=3 * 10**6, transcendentals=221184),
         name="ffn_pair",
     )(primal.T, tangent.T, w_in, w_out.T, b_in, *tables)
+    return pl.pallas_call(
+        part_ways,
+        out_shape=[jax.ShapeDtypeStruct((16, 16, 320), bf)] * 2,
+        in_specs=[pl.BlockSpec(memory_space=pltpu.VMEM)],
+        out_specs=[pl.BlockSpec(memory_space=pltpu.VMEM)] * 2,
+        name="part_ways",
+    )(both_out)
 
 
 def solution(mesh):

time: 139 us -> 138 us (level)
  local copies, waits for them, and re-layouts: 2.34 us -> 0 us
    unnamed x4 -> x0, local copies, waits for them, and re-layouts: 2.34 us -> none
    pallas_call x1 -> x2, Pallas kernels: 136 us -> 137 us  [the longest x1 135 us: shards(): pl.pallas_call(kernel, out_shape=jax.ShapeDtypeStruct((2, 16, 16, 320), b...]
where the time goes in v6:
time: 138 us
  Pallas kernels  137 us (99%)
    pallas_call x1, Pallas kernels, shards(): pl.pallas_call(kernel, out_shape=jax.ShapeDtypeStruct((2, 16, 16, 320), b...  135 us

profile of v6, /device:TPU:1, one launch (start us, length us, event | category | flops | bytes accessed | tf_op | source)
XLA Modules:
  0.0 137.8 jit_solution(3612279429140009836)
XLA Ops:
  0.6 135.4 %ffn_pair.1.both = bf16[2,16,16,320]{3,2,1,0:T(8,128)(2,1)} custom-call(bf16[320,256]{1,0:T(8,128)(2,1)} %bitcast.7, bf16[320,256]{1,0:T(8,128)(2,1)} %bitcast.8, bf16[320,864]{1,0:T(8,128)(2,1)} %w_in.1, bf16[320,864]{1,0:T(8,128)(2,1)} %bitcast.6, f32[864]{0:T(1024)} %b_in.1, f32[40,128]{1,0:T(8,128)} %bitcast.9, f32[40,128]{1,0:T(8,128)} %bitcast.10, ...), custom_call_target="tpu_custom_call" | custom-call | flops 8999999488 | bytes 3000000 | tf_op jit(solution)/shard_map/ffn_pair/pallas_call | solution.py:436
  136.1 1.8 %part_ways.1 = (bf16[16,16,320]{2,1,0:T(8,128)(2,1)}, bf16[16,16,320]{2,1,0:T(8,128)(2,1)}) custom-call(bf16[2,16,16,320]{3,2,1,0:T(8,128)(2,1)} %ffn_pair.1.both), custom_call_target="tpu_custom_call" | custom-call | tf_op jit(solution)/shard_map/part_ways/pallas_call | solution.py:466
